TPU v7x, 128 devices: a whole 4x4x4 slice. The times are simulated.
128 devices in a mesh: rows: 8 (over z, core), panel: 16 (over x, y).
Axes of the slice: x: 4, y: 4, z: 4, core: 2. Of those that a mesh axis runs over, the one named last changes fastest.
Arguments:
- weights: float32 [8192, 7168], P('rows', 'panel'), may hold values from -0.12 to 0.12
- grad: bfloat16 [8192, 7168], P('rows', 'panel'), may hold values from -6 to 6
- moment_first: float32 [8192, 7168], P('rows', 'panel'), may hold values from -3 to 3
- moment_second: float32 [8192, 7168], P('rows', 'panel'), may hold values from 0.1 to 4
- basis: bfloat16 [7168, 7168], P(None, 'panel'), may hold values from -0.0625 to 0.0625
- touched: int32 [64], P('rows'), may hold values from 0 to 1, as said below
Outputs:
- weights_new: float32 [8192, 7168], P('rows', 'panel')
- first_new: float32 [8192, 7168], P('rows', 'panel')
- second_new: float32 [8192, 7168], P('rows', 'panel')
- direction: float32 [8192, 7168], P('rows', 'panel')
Inputs may be any that keep to these rules, and one draw needn't show every extreme that they name: Each group of 8 consecutive blocks (those of one index of rows) has between 1 and 4 touched blocks, and some group has exactly 4.
All inputs are finite; a program needn't handle non-finite values.
Results may differ from a plain program's by a relative error of at most 0.015.
Values may be sent and summed in bfloat16 or wider, within the bound.
A program may use at most 128 MiB of HBM per device.

v0:
```python
import jax
import jax.numpy as jnp
from jax import lax
from jax.sharding import PartitionSpec as P

BLK = 128


beta_one = 0.95
correction = 1.0 - 0.95**10
epsilon = 1e-08
rate = 0.01


def advance(grad, first, second, basis, live):
    basis_rows = basis
    rotated = jnp.dot(
        lax.all_gather(grad, "panel", axis=1, tiled=True),
        basis_rows,
        preferred_element_type=jnp.float32,
    )
    first_new = jnp.where(live, beta_one * first + (1.0 - beta_one) * rotated, first)
    second_new = jnp.where(live, beta_one * second + (1.0 - beta_one) * rotated * rotated, second)
    ratio = first_new / correction / (jnp.sqrt(second_new / correction) + epsilon)
    normed = jnp.where(live, ratio, jnp.float32(0.0)).astype(jnp.bfloat16)
    basis_rows = basis
    summed = lax.psum_scatter(
        lax.dot_general(
            basis_rows, normed, (((1,), (1,)), ((), ())), preferred_element_type=jnp.float32
        ).astype(jnp.bfloat16),
        "panel",
        scatter_dimension=0,
        tiled=True,
    ).astype(jnp.float32)
    return (first_new, second_new, summed.T)


def per_device(weights, grad, moment_first, moment_second, basis, touched):
    live_rows = jnp.repeat(touched, BLK)[:, None] > 0
    first_new, second_new, direction = advance(grad, moment_first, moment_second, basis, live_rows)
    weights_new = weights - rate * direction
    return (weights_new, first_new, second_new, direction)


def solution(mesh):
    return jax.shard_map(
        per_device,
        mesh=mesh,
        in_specs=(
            P("rows", "panel"),
            P("rows", "panel"),
            P("rows", "panel"),
            P("rows", "panel"),
            P(None, "panel"),
            P("rows"),
        ),
        out_specs=(P("rows", "panel"), P("rows", "panel"), P("rows", "panel"), P("rows", "panel")),
        check_vma=False,
    )
```

profile of v0, /device:TPU:0, one launch (start us, length us, event | category | flops | bytes accessed | tf_op | source)
XLA Modules:
  0.0 280.1 jit_solution(16734692035392179797)
XLA Ops:
  7.2 0.0 all-gather.2.cloned.1.call-start
  7.2 0.7 all-gather.2.cloned.1.call-update
  7.9 0.0 reduce-scatter.4.cloned.1.call-start
  7.9 0.7 broadcast_compare_fusion
  8.6 0.1 broadcast_bitcast_fusion
  8.7 104.5 %all-gather.2.cloned.1.call-done = bf16[1024,7168]{0,1:T(8,128)(2,1)} async-done(((bf16[1024,448]{0,1:T(8,128)(2,1)}), bf16[1024,7168]{0,1:T(8,128)(2,1)}) %all-gather.2.cloned.1.call-update) | async-done | bytes 14680080 | tf_op jit(solution)/shard_map/all_gather | solution.py:18
  113.2 13.3 %fusion = (f32[1024,448]{0,1:T(8,128)S(1)}, f32[1024,448]{0,1:T(8,128)S(1)}) fusion(f32[1024,448]{0,1:T(8,128)} %param.8, pred[1024]{0:T(1024)(128)(4,1)S(1)} %broadcast_bitcast_fusion, f32[1024,448]{0,1:T(8,128)} %param.9, bf16[7168,448]{0,1:T(8,128)(2,1)} %param.10, bf16[1024,7168]{0,1:T(8,128)(2,1)} %all-gather.2.cloned.1.call-done), kind=kOutput, calls=%fused_computation.5 | convolution fusion | flops 6580338688 | bytes 28443648 | tf_op jit(solution)/shard_map/dot_general | solution.py:17
  126.5 0.0 copy-start.1
  126.5 0.0 copy-start.2
  126.5 1.2 copy-done.1
  127.7 0.6 copy-done.2
  128.3 14.4 %convert_bitcast_fusion = bf16[7168,1024]{0,1:T(8,128)(2,1)} fusion(bf16[7168,448]{0,1:T(8,128)(2,1)} %param.10, f32[1024,448]{0,1:T(8,128)S(1)} %get-tuple-element.13, f32[1024,448]{0,1:T(8,128)S(1)} %get-tuple-element.12, pred[1024]{0:T(1024)(128)(4,1)S(1)} %broadcast_bitcast_fusion), kind=kOutput, calls=%fused_computation | convolution fusion | flops 6586761216 | bytes 24773632 | tf_op jit(solution)/shard_map/dot_general | solution.py:28
  142.7 19.9 %copy.16 = bf16[7168,1024]{1,0:T(8,128)(2,1)} copy(bf16[7168,1024]{0,1:T(8,128)(2,1)} %convert_bitcast_fusion) | data formatting | bytes 29360128
  162.6 0.0 reduce-scatter.4.cloned.1.call-update
  162.6 1.9 copy.13
  164.5 99.3 %reduce-scatter.4.cloned.1.call-done = bf16[448,1024]{1,0:T(8,128)(2,1)} async-done(((bf16[7168,1024]{1,0:T(8,128)(2,1)}), bf16[448,1024]{1,0:T(8,128)(2,1)}) %reduce-scatter.4.cloned.1.call-update) | async-done | bytes 917520
  263.8 1.5 copy.17
  265.3 1.6 convert_bitcast_fusion.1
  266.9 1.7 multiply_subtract_fusion
  268.6 0.0 copy-start
  268.6 2.9 %copy.14 = f32[1024,448]{0,1:T(8,128)} copy(f32[1024,448]{1,0:T(8,128)} %multiply_subtract_fusion) | data formatting | bytes 3670016
  271.5 0.0 copy-done
  271.5 1.7 copy.15
Async XLA Ops:
  7.2 106.0 %all-gather.2.cloned.1.call-start = ((), (), s32[]{:S(2)}) async-start(), calls=%async_computation.1 | async-start | bytes 15597568 | tf_op jit(solution)/shard_map/all_gather | solution.py:18
  7.9 255.9 %reduce-scatter.4.cloned.1.call-start = ((), (), s32[]{:S(2)}) async-start(), calls=%async_computation.2 | async-start | bytes 15597568
  126.5 1.2 copy-start.1
  126.5 1.8 copy-start.2
  268.6 3.0 %copy-start = (f32[1024,448]{1,0:T(8,128)S(1)}, f32[1024,448]{1,0:T(8,128)}, u32[]{:S(2)}) copy-start(f32[1024,448]{1,0:T(8,128)} %convert_bitcast_fusion.1) | copy-start | bytes 5505028
Sparse Core Ops, SparseCore 0:
  10.2 102.9 all-gather.1
  162.7 101.0 reduce-scatter.3
where the time goes:
time: 281 us; the launch traced here: 280 us
  waiting for transfers between devices  205 us (73%)
  local copies, waits for them, and re-layouts  29.8 us (11%)
  matrix products  27.7 us (10%)
  between operations  14.1 us (5%)
  other arithmetic  3.96 us (1%)
    all_gather x1, waiting for transfers between devices, advance(): lax.all_gather(grad, 'panel', axis=1, tiled=True)  104 us
    unnamed x3, waiting for transfers between devices  100 us
    unnamed x11, local copies, waits for them, and re-layouts  29.7 us
    dot_general x1, matrix products, advance(): lax.dot_general(basis_rows, normed, (((1,), (1,)), ((), ())), preferred_e...  14.4 us
    dot_general x1, matrix products, advance(): jnp.dot(lax.all_gather(grad, 'panel', axis=1, tiled=True), basis_rows, pr...  13.3 us
  transfers between devices with their start and end apart: 2, of which 2 were waited for; matrix products, arithmetic and copies ran while one was open for 1% of the time, Pallas kernels for 0%

commit v1 on v0

v1 whole, which is shorter than its diff:
```python
import jax
import jax.numpy as jnp
from jax import lax
from jax.experimental import pallas as pl
from jax.experimental.pallas import tpu as pltpu
from jax.sharding import PartitionSpec as P

MESH = pl.DeviceIdType.MESH
BLK = 128
GRP = 8
SLOTS = 4
RING = 4
W = 448
K = RING * W
HALF = W // 2
PART = W // 4
KPART = K // 2
DIRECT = 48
VIA = (PART - DIRECT) // 2
PAIR = 2

beta_one = 0.95
correction = 1.0 - 0.95**10
epsilon = 1e-08
rate = 0.01


def slot_of_block(touched):
    slots = []
    seen = jnp.int32(0)
    for b in range(GRP):
        on = jnp.minimum(touched[b], 1)
        slots.append(on * (seen + 1) - 1)
        seen = seen + on
    return slots


def live_block(slots, slot, ref):
    found = ref[:, 0:BLK]
    for b in range(1, GRP):
        here = jnp.broadcast_to(slots[b], found.shape) == slot
        found = jnp.where(here, ref[:, b * BLK:(b + 1) * BLK], found)
    return found


def exchange(touched, grad_hbm, first_hbm, second_hbm, basis_hbm, rot_out, dir_out,
             grad_v, first_v, second_v, first_c, second_c, basis_v, gw, nw, own_v, back_v,
             xs2, xa, xs, xr, ys2, ya, ys, yr,
             load_sem,
             bx_s, bx_r, bz_s, bz_r, bf_s, bf_r, bc_s, bc_r,
             gy_s, gy_r, nx_s, nx_r, rx_s, rx_r, ry_s, ry_r):
    r, p = lax.axis_index("rows"), lax.axis_index("panel")
    z, c = r // 2, lax.rem(r, 2)
    x, y = p // RING, lax.rem(p, RING)

    def device(dz=0, dc=0, dx=0, dy=0):
        return (lax.rem(z + dz, 4) * 2 + lax.rem(c + dc, 2), lax.rem(x + dx, RING) * RING + lax.rem(y + dy, RING))

    def remote(src, dst, send, recv, to):
        return pltpu.make_async_remote_copy(
            src_ref=src, dst_ref=dst, send_sem=send, recv_sem=recv, device_id=to, device_id_type=MESH)

    xp, xm, x2 = device(dx=1), device(dx=3), device(dx=2)
    yp, ym = device(dy=1), device(dy=3)
    zp, zm, other = device(dz=1), device(dz=3), device(dc=1)

    barrier = pltpu.get_barrier_semaphore()
    peers = (xp, xm, x2, yp, ym, zp, zm, other)
    for peer in peers:
        pl.semaphore_signal(barrier, inc=1, device_id=peer, device_id_type=MESH)

    own_rows = pl.ds(pl.multiple_of(x * K, 128), K)
    loads = [pltpu.make_async_copy(grad_hbm, grad_v, load_sem.at[0]),
             pltpu.make_async_copy(basis_hbm.at[:, own_rows], basis_v.at[x], load_sem.at[1]),
             pltpu.make_async_copy(first_hbm, first_v, load_sem.at[2]),
             pltpu.make_async_copy(second_hbm, second_v, load_sem.at[3])]
    for load in loads:
        load.start()

    loads[0].wait()
    slots = slot_of_block(touched)
    for s in range(SLOTS):
        gw[s, y] = live_block(slots, s, grad_v)

    pl.semaphore_wait(barrier, len(peers))

    def ring_of(at, d):
        return lax.rem(at + d, RING)

    def part(panel, k, core, low=0, size=PART):
        rows = pl.ds(pl.multiple_of(ring_of(z, k) * PART + low, 16), size)
        return basis_v.at[panel, rows, pl.ds(pl.multiple_of(core * KPART, 128), KPART)]

    def bx(dx, k):
        size = PART if k == 0 else DIRECT
        rows = pl.ds(pl.multiple_of(ring_of(z, k) * PART, 16), size)
        cols = pl.ds(pl.multiple_of(ring_of(x, dx) * K + c * KPART, 128), KPART)
        return remote(basis_hbm.at[rows, cols], part(x, k, c, 0, size), bx_s.at[dx - 1, k // 2],
                      bx_r.at[3 - dx, k // 2], {1: xp, 2: x2, 3: xm}[dx])

    def bx_in(d, k):
        piece = part(ring_of(x, d), k, c, 0, PART if k == 0 else DIRECT)
        return remote(piece, piece, bx_s.at[3 - d, k // 2], bx_r.at[d - 1, k // 2], xp)

    def bz(d, up):
        piece = part(ring_of(x, d), 0, c)
        return remote(piece, piece, bz_s.at[d - 1, up], bz_r.at[d - 1, up], zp if up else zm)

    def bz_in(d, up):
        piece = part(ring_of(x, d), 3 if up else 1, c)
        return remote(piece, piece, bz_s.at[d - 1, up], bz_r.at[d - 1, up], zp if up else zm)

    def bf(d, up):
        piece = part(ring_of(x, d), 3 if up else 1, c, DIRECT + up * VIA, VIA)
        return remote(piece, piece, bf_s.at[d - 1, up], bf_r.at[d - 1, up], zp if up else zm)

    def bf_in(d, up):
        piece = part(ring_of(x, d), 2, c, DIRECT + up * VIA, VIA)
        return remote(piece, piece, bf_s.at[d - 1, up], bf_r.at[d - 1, up], zp if up else zm)

    def bc(d, k):
        piece = part(ring_of(x, d), k, c)
        return remote(piece, piece, bc_s.at[d - 1, k], bc_r.at[d - 1, k], other)

    def bc_in(d, k):
        piece = part(ring_of(x, d), k, 1 - c)
        return remote(piece, piece, bc_s.at[d - 1, k], bc_r.at[d - 1, k], other)

    def ag(w, me, send, recv, plus, minus):
        def copy(j, up, block, low, size, n):
            piece = w.at[j, block, pl.ds(low, size)]
            return remote(piece, piece, send.at[n + up, j], recv.at[n + up, j], plus if up else minus)

        def own(j, up):
            return copy(j, up, me, 0, W, 0)

        def own_in(j, up):
            return copy(j, up, ring_of(me, 3 if up else 1), 0, W, 0)

        def onward(j, up):
            return copy(j, up, ring_of(me, 3 if up else 1), up * HALF, HALF, 2)

        def onward_in(j, up):
            return copy(j, up, ring_of(me, 2), up * HALF, HALF, 2)

        return own, own_in, onward, onward_in

    def rs(s2, a, s, t, send, recv, plus, minus):
        def far(j, up):
            return remote(s2.at[j, pl.ds(up * HALF, HALF)], a.at[up, j], send.at[up, j], recv.at[up, j],
                          plus if up else minus)

        def near(j, up):
            return remote(s.at[up, j], t.at[up, j], send.at[2 + up, j], recv.at[2 + up, j], plus if up else minus)

        return far, near

    g_own, g_own_in, g_on, g_on_in = ag(gw, y, gy_s, gy_r, yp, ym)
    n_own, n_own_in, n_on, n_on_in = ag(nw, x, nx_s, nx_r, xp, xm)
    x_far, x_near = rs(xs2, xa, xs, xr, rx_s, rx_r, xp, xm)
    y_far, y_near = rs(ys2, ya, ys, yr, ry_s, ry_r, yp, ym)

    def loop(body, n=SLOTS):
        def step(j, carry):
            body(j)
            return carry

        lax.fori_loop(0, n, step, 0)

    for dx in (2, 1, 3):
        for k in (0, 2):
            bx(dx, k).start()

    def send_g(j):
        g_own(j, 1).start()
        g_own(j, 0).start()

    loop(send_g)

    def pass_on(d):
        bx_in(d, 0).wait_recv()
        bz(d, 1).start()
        bz(d, 0).start()
        bc(d, 0).start()

    def pass_round(d):
        bz_in(d, 0).wait_recv()
        bf(d, 0).start()
        bz_in(d, 1).wait_recv()
        bf(d, 1).start()
        bc(d, 1).start()
        bc(d, 3).start()

    def pass_last(d):
        bx_in(d, 2).wait_recv()
        bf_in(d, 0).wait_recv()
        bf_in(d, 1).wait_recv()
        bc(d, 2).start()

    def whole(d):
        for k in range(4):
            bc_in(d, k).wait_recv()

    def forward_g(j):
        g_own_in(j, 0).wait_recv()
        g_on(j, 0).start()
        g_own_in(j, 1).wait_recv()
        g_on(j, 1).start()

    def arrived_g(j):
        g_on_in(j, 0).wait_recv()
        g_on_in(j, 1).wait_recv()

    def rotate(d, i):
        rows = jnp.concatenate([gw[i * PAIR + t].reshape(K, BLK) for t in range(PAIR)], axis=1)
        return jnp.dot(basis_v[ring_of(x, d)], rows, preferred_element_type=jnp.float32)

    def send_far(term, s2, far, j):
        s2[j] = term.astype(jnp.bfloat16)
        far(j, 0).start()
        far(j, 1).start()

    def send_near(term, up, a, s, far, near, j):
        far(j, up).wait_recv()
        came = a[up, j].astype(jnp.float32)
        low, high = term[:HALF], term[HALF:]
        s[up, j, 0:HALF] = (low if up else low + came).astype(jnp.bfloat16)
        s[up, j, HALF:W] = (high + came if up else high).astype(jnp.bfloat16)
        near(j, up).start()

    def finish(term, t, near, j):
        near(j, 0).wait_recv()
        near(j, 1).wait_recv()
        return term + t[0, j].astype(jnp.float32) + t[1, j].astype(jnp.float32)

    pass_on(2)
    loads[2].wait()
    loads[3].wait()
    for s in range(SLOTS):
        first_c[s] = live_block(slots, s, first_v)
        second_c[s] = live_block(slots, s, second_v)
    loop(forward_g)
    pass_round(2)
    pass_on(1)
    pass_on(3)
    pass_last(2)
    pass_round(1)
    pass_round(3)
    loads[1].wait()
    whole(2)

    def step_far(i):
        for t in range(PAIR):
            arrived_g(i * PAIR + t)
        share = rotate(2, i)
        for t in range(PAIR):
            send_far(share[:, t * BLK:(t + 1) * BLK], xs2, x_far, i * PAIR + t)
        share = rotate(0, i)
        for t in range(PAIR):
            own_v[i * PAIR + t] = share[:, t * BLK:(t + 1) * BLK]

    loop(step_far, SLOTS // PAIR)
    pass_last(1)
    pass_last(3)
    whole(3)
    whole(1)

    def step_near(i):
        for d, up in ((3, 0), (1, 1)):
            share = rotate(d, i)
            for t in range(PAIR):
                send_near(share[:, t * BLK:(t + 1) * BLK], up, xa, xs, x_far, x_near, i * PAIR + t)

    loop(step_near, SLOTS // PAIR)

    def normalise(j):
        rotated = finish(own_v[j], xr, x_near, j)
        rot_out[j] = rotated
        first_new = beta_one * first_c[j] + (1.0 - beta_one) * rotated
        second_new = beta_one * second_c[j] + (1.0 - beta_one) * rotated * rotated
        ratio = first_new / correction / (jnp.sqrt(second_new / correction) + epsilon)
        nw[j, x] = ratio.astype(jnp.bfloat16)
        n_own(j, 1).start()
        n_own(j, 0).start()

    def forward_n(j):
        n_own_in(j, 0).wait_recv()
        n_on(j, 0).start()
        n_own_in(j, 1).wait_recv()
        n_on(j, 1).start()

    def back_far(j):
        n_on_in(j, 0).wait_recv()
        n_on_in(j, 1).wait_recv()
        total = None
        for d in range(RING):
            term = jnp.dot(nw[j, d].T, basis_v[d], preferred_element_type=jnp.float32)
            total = term if total is None else total + term
        back_v[j] = total.T.reshape(RING, W, BLK)
        send_far(back_v[j, ring_of(y, 2)], ys2, y_far, j)

    def back_near(j):
        send_near(back_v[j, ring_of(y, 3)], 0, ya, ys, y_far, y_near, j)
        send_near(back_v[j, ring_of(y, 1)], 1, ya, ys, y_far, y_near, j)

    def back_own(j):
        dir_out[j] = finish(back_v[j, y], yr, y_near, j)

    tasks = (normalise, forward_n, back_far, back_near, back_own)

    def skewed(t):
        for lag, task in enumerate(tasks):
            j = t - lag

            @pl.when((j >= 0) & (j < SLOTS))
            def _():
                task(j)

    loop(skewed, SLOTS + len(tasks) - 1)

    for d in (2, 1, 3):
        for k in (0, 2):
            bx(d, k).wait_send()
        for up in (0, 1):
            bz(d, up).wait_send()
            bf(d, up).wait_send()
        for k in range(4):
            bc(d, k).wait_send()

    def drain(j):
        for up in (0, 1):
            for copy in (g_own, g_on, n_own, n_on, x_far, x_near, y_far, y_near):
                copy(j, up).wait_send()

    loop(drain)


def call_exchange(touched, grad, first, second, basis):
    bf16, f32 = jnp.bfloat16, jnp.float32
    any_space = pl.BlockSpec(memory_space=pl.ANY)
    vmem = pl.BlockSpec(memory_space=pltpu.VMEM)

    def sum_buffers():
        return [pltpu.VMEM((SLOTS, W, BLK), bf16), pltpu.VMEM((2, SLOTS, HALF, BLK), bf16),
                pltpu.VMEM((2, SLOTS, W, BLK), bf16), pltpu.VMEM((2, SLOTS, W, BLK), bf16)]

    def sems(*shape):
        return [pltpu.SemaphoreType.DMA(shape), pltpu.SemaphoreType.DMA(shape)]

    scratch = [
        pltpu.VMEM((W, GRP * BLK), bf16), pltpu.VMEM((W, GRP * BLK), f32), pltpu.VMEM((W, GRP * BLK), f32),
        pltpu.VMEM((SLOTS, W, BLK), f32), pltpu.VMEM((SLOTS, W, BLK), f32),
        pltpu.VMEM((RING, W, K), bf16),
        pltpu.VMEM((SLOTS, RING, W, BLK), bf16), pltpu.VMEM((SLOTS, RING, W, BLK), bf16),
        pltpu.VMEM((SLOTS, W, BLK), f32), pltpu.VMEM((SLOTS, RING, W, BLK), f32),
        *sum_buffers(), *sum_buffers(),
        pltpu.SemaphoreType.DMA((4,)),
        *sems(3, 2), *sems(3, 2), *sems(3, 2), *sems(3, 4),
        *sems(4, SLOTS), *sems(4, SLOTS), *sems(4, SLOTS), *sems(4, SLOTS),
    ]
    compact = jax.ShapeDtypeStruct((SLOTS, W, BLK), f32)
    return pl.pallas_call(
        exchange,
        out_shape=(compact, compact),
        in_specs=[pl.BlockSpec(memory_space=pltpu.SMEM)] + [any_space] * 4,
        out_specs=(vmem, vmem),
        scratch_shapes=scratch,
        compiler_params=pltpu.CompilerParams(
            collective_id=0, has_side_effects=True, vmem_limit_bytes=56 * 2**20),
        cost_estimate=pl.CostEstimate(flops=4 * SLOTS * BLK * K * K, bytes_accessed=16 * 2**20, transcendentals=0),
        name="exchange",
    )(touched, grad, first, second, basis)


def store(touched, rot, direction, weights, first, second, weights_new, first_new, second_new, direction_new):
    live = touched[pl.program_id(0)] > 0
    rotated = rot[0]
    old_first, old_second = first[...], second[...]
    first_new[...] = jnp.where(live, beta_one * old_first + (1.0 - beta_one) * rotated, old_first)
    second_new[...] = jnp.where(live, beta_one * old_second + (1.0 - beta_one) * rotated * rotated, old_second)
    step = jnp.where(live, direction[0], 0.0)
    direction_new[...] = step
    weights_new[...] = weights[...] - rate * step


def call_store(touched, rot, direction, weights, first, second):
    def slot(b, touched):
        seen = jnp.int32(0)
        for i in range(GRP - 1):
            seen = seen + jnp.where((i < b) & (touched[i] > 0), jnp.int32(1), jnp.int32(0))
        return jnp.minimum(seen, SLOTS - 1), 0, 0

    compact = pl.BlockSpec((1, W, BLK), slot)
    block = pl.BlockSpec((W, BLK), lambda b, touched: (0, b))
    full = jax.ShapeDtypeStruct((W, GRP * BLK), jnp.float32)
    return pl.pallas_call(
        store,
        out_shape=(full,) * 4,
        grid_spec=pltpu.PrefetchScalarGridSpec(
            num_scalar_prefetch=1, grid=(GRP,), in_specs=[compact] * 2 + [block] * 3, out_specs=[block] * 4),
        name="store",
    )(touched, rot, direction, weights, first, second)


def per_device(weights, grad, moment_first, moment_second, basis, touched):
    weights, grad, first, second, basis = (a.T for a in (weights, grad, moment_first, moment_second, basis))
    rot, direction = call_exchange(touched, grad, first, second, basis)
    return tuple(a.T for a in call_store(touched, rot, direction, weights, first, second))


def solution(mesh):
    spec = P("rows", "panel")
    return jax.shard_map(
        per_device,
        mesh=mesh,
        in_specs=(spec, spec, spec, spec, P(None, "panel"), P("rows")),
        out_specs=(spec,) * 4,
        check_vma=False,
    )
```

time: 281 us -> 93.3 us (0.33)
  waiting for transfers between devices: 205 us -> 0 us
  Pallas kernels: 0 us -> 92.3 us
  local copies, waits for them, and re-layouts: 29.8 us -> 0 us
  matrix products: 27.7 us -> 0 us
  between operations: 14.1 us -> 0.64 us
  other arithmetic: 3.96 us -> 0 us
    all_gather x1 -> x0, waiting for transfers between devices: 104 us -> none  [advance(): lax.all_gather(grad, 'panel', axis=1, tiled=True)]
    unnamed x3 -> x0, waiting for transfers between devices: 100 us -> none
    pallas_call x0 -> x2, Pallas kernels: none -> 92.3 us  [the longest x1 83.1 us: call_exchange(): pl.pallas_call(exchange, out_shape=(compact, compact), in_specs=[pl.Block...]
    unnamed x11 -> x0, local copies, waits for them, and re-layouts: 29.7 us -> none
    dot_general x2 -> x0, matrix products: 27.7 us -> none  [the longest x1 14.4 us: advance(): lax.dot_general(basis_rows, normed, (((1,), (1,)), ((), ())), preferred_e...]
  transfers between devices with their start and end apart: 2 -> 0, of which waited for: 2 -> 0; matrix products, arithmetic and copies ran while one was open for 1% -> 0% of each run, Pallas kernels for 0% -> 0%
where the time goes in v1:
time: 93.3 us; the launch traced here: 93 us
  Pallas kernels  92.3 us (99%)
    pallas_call x1, Pallas kernels, call_exchange(): pl.pallas_call(exchange, out_shape=(compact, compact), in_specs=[pl.Block...  83.1 us
    pallas_call x1, Pallas kernels, call_store(): pl.pallas_call(store, out_shape=(full,) * 4, grid_spec=pltpu.PrefetchScal...  9.29 us

profile of v1, /device:TPU:0, one launch (start us, length us, event | category | flops | bytes accessed | tf_op | source)
XLA Modules:
  0.0 93.0 jit_solution(12436194320105612086)
XLA Ops:
  0.6 83.1 %exchange.1 = (f32[4,448,128]{2,1,0:T(8,128)}, f32[4,448,128]{2,1,0:T(8,128)}) custom-call(s32[8]{0:T(128)} %touched.3, bf16[448,1024]{1,0:T(8,128)(2,1)} %bitcast.19, f32[448,1024]{1,0:T(8,128)} %bitcast.9, f32[448,1024]{1,0:T(8,128)} %bitcast.11, bf16[448,7168]{1,0:T(8,128)(2,1)} %bitcast.14), custom_call_target="tpu_custom_call" | custom-call | flops 6576668672 | bytes 16777216 | tf_op jit(solution)/shard_map/exchange/pallas_call | solution.py:362
  83.7 9.3 %store.1 = (f32[448,1024]{1,0:T(8,128)}, f32[448,1024]{1,0:T(8,128)}, f32[448,1024]{1,0:T(8,128)}, f32[448,1024]{1,0:T(8,128)}) custom-call(s32[8]{0:T(128)} %touched.3, f32[4,448,128]{2,1,0:T(8,128)} %get-tuple-element.10.rot, f32[4,448,128]{2,1,0:T(8,128)} %get-tuple-element.11.direction, f32[448,1024]{1,0:T(8,128)} %bitcast.13, f32[448,1024]{1,0:T(8,128)} %bitcast.10, ...), custom_call_target="tpu_custom_call" | custom-call | tf_op jit(solution)/shard_map/store/pallas_call | solution.py:396

commit v2 on v1

--- a/solution.py
+++ b/solution.py
@@ -15,9 +15,11 @@
 HALF = W // 2
 PART = W // 4
 KPART = K // 2
-DIRECT = 48
+DIRECT = 80
 VIA = (PART - DIRECT) // 2
+SUBS = ((0, 64), (64, 48))
 PAIR = 2
+STRIP = 64
 
 beta_one = 0.95
 correction = 1.0 - 0.95**10
@@ -74,15 +76,8 @@
              pltpu.make_async_copy(basis_hbm.at[:, own_rows], basis_v.at[x], load_sem.at[1]),
              pltpu.make_async_copy(first_hbm, first_v, load_sem.at[2]),
              pltpu.make_async_copy(second_hbm, second_v, load_sem.at[3])]
-    for load in loads:
-        load.start()
-
-    loads[0].wait()
+    loads[0].start()
     slots = slot_of_block(touched)
-    for s in range(SLOTS):
-        gw[s, y] = live_block(slots, s, grad_v)
-
-    pl.semaphore_wait(barrier, len(peers))
 
     def ring_of(at, d):
         return lax.rem(at + d, RING)
@@ -91,24 +86,28 @@
         rows = pl.ds(pl.multiple_of(ring_of(z, k) * PART + low, 16), size)
         return basis_v.at[panel, rows, pl.ds(pl.multiple_of(core * KPART, 128), KPART)]
 
-    def bx(dx, k):
-        size = PART if k == 0 else DIRECT
-        rows = pl.ds(pl.multiple_of(ring_of(z, k) * PART, 16), size)
+    def span(n):
+        return (0, *SUBS[n]) if n < 2 else (2, 0, DIRECT)
+
+    def bx(dx, n):
+        k, low, size = span(n)
+        rows = pl.ds(pl.multiple_of(ring_of(z, k) * PART + low, 16), size)
         cols = pl.ds(pl.multiple_of(ring_of(x, dx) * K + c * KPART, 128), KPART)
-        return remote(basis_hbm.at[rows, cols], part(x, k, c, 0, size), bx_s.at[dx - 1, k // 2],
-                      bx_r.at[3 - dx, k // 2], {1: xp, 2: x2, 3: xm}[dx])
-
-    def bx_in(d, k):
-        piece = part(ring_of(x, d), k, c, 0, PART if k == 0 else DIRECT)
-        return remote(piece, piece, bx_s.at[3 - d, k // 2], bx_r.at[d - 1, k // 2], xp)
-
-    def bz(d, up):
-        piece = part(ring_of(x, d), 0, c)
-        return remote(piece, piece, bz_s.at[d - 1, up], bz_r.at[d - 1, up], zp if up else zm)
-
-    def bz_in(d, up):
-        piece = part(ring_of(x, d), 3 if up else 1, c)
-        return remote(piece, piece, bz_s.at[d - 1, up], bz_r.at[d - 1, up], zp if up else zm)
+        return remote(basis_hbm.at[rows, cols], part(x, k, c, low, size), bx_s.at[dx - 1, n],
+                      bx_r.at[3 - dx, n], {1: xp, 2: x2, 3: xm}[dx])
+
+    def bx_in(d, n):
+        k, low, size = span(n)
+        piece = part(ring_of(x, d), k, c, low, size)
+        return remote(piece, piece, bx_s.at[3 - d, n], bx_r.at[d - 1, n], xp)
+
+    def bz(d, up, n):
+        piece = part(ring_of(x, d), 0, c, *SUBS[n])
+        return remote(piece, piece, bz_s.at[d - 1, up, n], bz_r.at[d - 1, up, n], zp if up else zm)
+
+    def bz_in(d, up, n):
+        piece = part(ring_of(x, d), 3 if up else 1, c, *SUBS[n])
+        return remote(piece, piece, bz_s.at[d - 1, up, n], bz_r.at[d - 1, up, n], zp if up else zm)
 
     def bf(d, up):
         piece = part(ring_of(x, d), 3 if up else 1, c, DIRECT + up * VIA, VIA)
@@ -118,13 +117,16 @@
         piece = part(ring_of(x, d), 2, c, DIRECT + up * VIA, VIA)
         return remote(piece, piece, bf_s.at[d - 1, up], bf_r.at[d - 1, up], zp if up else zm)
 
-    def bc(d, k):
-        piece = part(ring_of(x, d), k, c)
-        return remote(piece, piece, bc_s.at[d - 1, k], bc_r.at[d - 1, k], other)
-
-    def bc_in(d, k):
-        piece = part(ring_of(x, d), k, 1 - c)
-        return remote(piece, piece, bc_s.at[d - 1, k], bc_r.at[d - 1, k], other)
+    def bc_span(k, n):
+        return (0, PART) if k == 2 else SUBS[n]
+
+    def bc(d, k, n=0):
+        piece = part(ring_of(x, d), k, c, *bc_span(k, n))
+        return remote(piece, piece, bc_s.at[d - 1, k, n], bc_r.at[d - 1, k, n], other)
+
+    def bc_in(d, k, n=0):
+        piece = part(ring_of(x, d), k, 1 - c, *bc_span(k, n))
+        return remote(piece, piece, bc_s.at[d - 1, k, n], bc_r.at[d - 1, k, n], other)
 
     def ag(w, me, send, recv, plus, minus):
         def copy(j, up, block, low, size, n):
@@ -150,8 +152,10 @@
             return remote(s2.at[j, pl.ds(up * HALF, HALF)], a.at[up, j], send.at[up, j], recv.at[up, j],
                           plus if up else minus)
 
-        def near(j, up):
-            return remote(s.at[up, j], t.at[up, j], send.at[2 + up, j], recv.at[2 + up, j], plus if up else minus)
+        def near(j, up, summed):
+            rows = pl.ds((up if summed else 1 - up) * HALF, HALF)
+            n = 2 + 2 * summed + up
+            return remote(s.at[up, j, rows], t.at[up, j, rows], send.at[n, j], recv.at[n, j], plus if up else minus)
 
         return far, near
 
@@ -167,29 +171,34 @@
 
         lax.fori_loop(0, n, step, 0)
 
-    for dx in (2, 1, 3):
-        for k in (0, 2):
-            bx(dx, k).start()
+    pl.semaphore_wait(barrier, len(peers))
+    for dx, n in ((2, 0), (2, 1), (1, 0), (3, 0), (1, 1), (3, 1)):
+        bx(dx, n).start()
 
     def send_g(j):
         g_own(j, 1).start()
         g_own(j, 0).start()
 
-    loop(send_g)
-
-    def pass_on(d):
-        bx_in(d, 0).wait_recv()
-        bz(d, 1).start()
-        bz(d, 0).start()
-        bc(d, 0).start()
-
-    def pass_round(d):
-        bz_in(d, 0).wait_recv()
-        bf(d, 0).start()
-        bz_in(d, 1).wait_recv()
-        bf(d, 1).start()
-        bc(d, 1).start()
-        bc(d, 3).start()
+    loads[0].wait()
+    for j in range(SLOTS):
+        gw[j, y] = live_block(slots, j, grad_v)
+        if j < PAIR:
+            send_g(j)
+    for load in loads[1:]:
+        load.start()
+
+    def pass_on(d, n):
+        bx_in(d, n).wait_recv()
+        bz(d, 1, n).start()
+        bz(d, 0, n).start()
+        bc(d, 0, n).start()
+
+    def pass_round(d, n):
+        for up, k in ((0, 1), (1, 3)):
+            bz_in(d, up, n).wait_recv()
+            if n:
+                bf(d, up).start()
+            bc(d, k, n).start()
 
     def pass_last(d):
         bx_in(d, 2).wait_recv()
@@ -198,8 +207,10 @@
         bc(d, 2).start()
 
     def whole(d):
-        for k in range(4):
-            bc_in(d, k).wait_recv()
+        for n in (0, 1):
+            for k in (0, 1, 3):
+                bc_in(d, k, n).wait_recv()
+        bc_in(d, 2).wait_recv()
 
     def forward_g(j):
         g_own_in(j, 0).wait_recv()
@@ -220,32 +231,47 @@
         far(j, 0).start()
         far(j, 1).start()
 
-    def send_near(term, up, a, s, far, near, j):
+    def send_ready(term, up, s, near, j):
+        rows = slice(0, HALF) if up else slice(HALF, W)
+        s[up, j, rows] = term[rows].astype(jnp.bfloat16)
+        near(j, up, 0).start()
+
+    def send_summed(term, up, a, s, far, near, j):
+        rows = slice(HALF, W) if up else slice(0, HALF)
         far(j, up).wait_recv()
-        came = a[up, j].astype(jnp.float32)
-        low, high = term[:HALF], term[HALF:]
-        s[up, j, 0:HALF] = (low if up else low + came).astype(jnp.bfloat16)
-        s[up, j, HALF:W] = (high + came if up else high).astype(jnp.bfloat16)
-        near(j, up).start()
+        s[up, j, rows] = (term[rows] + a[up, j].astype(jnp.float32)).astype(jnp.bfloat16)
+        near(j, up, 1).start()
 
     def finish(term, t, near, j):
-        near(j, 0).wait_recv()
-        near(j, 1).wait_recv()
+        for up in (0, 1):
+            near(j, up, 0).wait_recv()
+            near(j, up, 1).wait_recv()
         return term + t[0, j].astype(jnp.float32) + t[1, j].astype(jnp.float32)
 
-    pass_on(2)
-    loads[2].wait()
-    loads[3].wait()
-    for s in range(SLOTS):
-        first_c[s] = live_block(slots, s, first_v)
-        second_c[s] = live_block(slots, s, second_v)
-    loop(forward_g)
-    pass_round(2)
-    pass_on(1)
-    pass_on(3)
+    pass_on(2, 0)
+    forward_g(0)
+    send_g(2)
+    pass_on(2, 1)
+    forward_g(1)
+    send_g(3)
+    for load in loads[2:]:
+        load.wait()
+    for j in range(SLOTS):
+        first_c[j] = live_block(slots, j, first_v)
+        second_c[j] = live_block(slots, j, second_v)
+    pass_on(3, 0)
+    pass_on(1, 0)
+    pass_round(2, 0)
+    pass_round(2, 1)
+    for dx in (2, 1, 3):
+        bx(dx, 2).start()
+    pass_on(3, 1)
+    pass_on(1, 1)
+    forward_g(2)
+    forward_g(3)
     pass_last(2)
-    pass_round(1)
-    pass_round(3)
+    pass_round(3, 0)
+    pass_round(1, 0)
     loads[1].wait()
     whole(2)
 
@@ -260,6 +286,8 @@
             own_v[i * PAIR + t] = share[:, t * BLK:(t + 1) * BLK]
 
     loop(step_far, SLOTS // PAIR)
+    pass_round(3, 1)
+    pass_round(1, 1)
     pass_last(1)
     pass_last(3)
     whole(3)
@@ -269,7 +297,9 @@
         for d, up in ((3, 0), (1, 1)):
             share = rotate(d, i)
             for t in range(PAIR):
-                send_near(share[:, t * BLK:(t + 1) * BLK], up, xa, xs, x_far, x_near, i * PAIR + t)
+                send_ready(share[:, t * BLK:(t + 1) * BLK], up, xs, x_near, i * PAIR + t)
+            for t in range(PAIR):
+                send_summed(share[:, t * BLK:(t + 1) * BLK], up, xa, xs, x_far, x_near, i * PAIR + t)
 
     loop(step_near, SLOTS // PAIR)
 
@@ -298,10 +328,12 @@
             total = term if total is None else total + term
         back_v[j] = total.T.reshape(RING, W, BLK)
         send_far(back_v[j, ring_of(y, 2)], ys2, y_far, j)
+        send_ready(back_v[j, ring_of(y, 3)], 0, ys, y_near, j)
+        send_ready(back_v[j, ring_of(y, 1)], 1, ys, y_near, j)
 
     def back_near(j):
-        send_near(back_v[j, ring_of(y, 3)], 0, ya, ys, y_far, y_near, j)
-        send_near(back_v[j, ring_of(y, 1)], 1, ya, ys, y_far, y_near, j)
+        send_summed(back_v[j, ring_of(y, 3)], 0, ya, ys, y_far, y_near, j)
+        send_summed(back_v[j, ring_of(y, 1)], 1, ya, ys, y_far, y_near, j)
 
     def back_own(j):
         dir_out[j] = finish(back_v[j, y], yr, y_near, j)
@@ -319,18 +351,24 @@
     loop(skewed, SLOTS + len(tasks) - 1)
 
     for d in (2, 1, 3):
-        for k in (0, 2):
-            bx(d, k).wait_send()
+        for n in range(3):
+            bx(d, n).wait_send()
         for up in (0, 1):
-            bz(d, up).wait_send()
+            bz(d, up, 0).wait_send()
+            bz(d, up, 1).wait_send()
             bf(d, up).wait_send()
-        for k in range(4):
-            bc(d, k).wait_send()
+        for k in (0, 1, 3):
+            bc(d, k, 0).wait_send()
+            bc(d, k, 1).wait_send()
+        bc(d, 2).wait_send()
 
     def drain(j):
         for up in (0, 1):
-            for copy in (g_own, g_on, n_own, n_on, x_far, x_near, y_far, y_near):
+            for copy in (g_own, g_on, n_own, n_on, x_far, y_far):
                 copy(j, up).wait_send()
+            for copy in (x_near, y_near):
+                copy(j, up, 0).wait_send()
+                copy(j, up, 1).wait_send()
 
     loop(drain)
 
@@ -355,10 +393,10 @@
         pltpu.VMEM((SLOTS, W, BLK), f32), pltpu.VMEM((SLOTS, RING, W, BLK), f32),
         *sum_buffers(), *sum_buffers(),
         pltpu.SemaphoreType.DMA((4,)),
-        *sems(3, 2), *sems(3, 2), *sems(3, 2), *sems(3, 4),
-        *sems(4, SLOTS), *sems(4, SLOTS), *sems(4, SLOTS), *sems(4, SLOTS),
+        *sems(3, 3), *sems(3, 2, 2), *sems(3, 2), *sems(3, 4, 2),
+        *sems(4, SLOTS), *sems(4, SLOTS), *sems(6, SLOTS), *sems(6, SLOTS),
     ]
-    compact = jax.ShapeDtypeStruct((SLOTS, W, BLK), f32)
+    compact = pltpu.VMEM((SLOTS, W, BLK), f32)
     return pl.pallas_call(
         exchange,
         out_shape=(compact, compact),
@@ -372,32 +410,52 @@
     )(touched, grad, first, second, basis)
 
 
-def store(touched, rot, direction, weights, first, second, weights_new, first_new, second_new, direction_new):
-    live = touched[pl.program_id(0)] > 0
-    rotated = rot[0]
-    old_first, old_second = first[...], second[...]
-    first_new[...] = jnp.where(live, beta_one * old_first + (1.0 - beta_one) * rotated, old_first)
-    second_new[...] = jnp.where(live, beta_one * old_second + (1.0 - beta_one) * rotated * rotated, old_second)
-    step = jnp.where(live, direction[0], 0.0)
-    direction_new[...] = step
-    weights_new[...] = weights[...] - rate * step
+def store(touched, rot, direction, weights, first, second, weights_new, first_new, second_new, direction_new,
+          out_v, sems):
+    slots = []
+    seen = jnp.int32(0)
+    for b in range(GRP):
+        slots.append(jnp.minimum(seen, SLOTS - 1))
+        seen = seen + touched[b]
+    outs = (weights_new, first_new, second_new, direction_new)
+
+    def copies(i):
+        rows = pl.ds(pl.multiple_of(i * STRIP, 8), STRIP)
+        return [pltpu.make_async_copy(out_v.at[o, rows], outs[o].at[rows], sems.at[o, i]) for o in range(4)]
+
+    def strip(i, carry):
+        rows = pl.ds(pl.multiple_of(i * STRIP, 8), STRIP)
+        for b in range(GRP):
+            cols = slice(b * BLK, (b + 1) * BLK)
+            live = touched[b] > 0
+            rotated = rot[slots[b], rows]
+            old_first, old_second = first[rows, cols], second[rows, cols]
+            step = jnp.where(live, direction[slots[b], rows], 0.0)
+            out_v[0, rows, cols] = weights[rows, cols] - rate * step
+            out_v[1, rows, cols] = jnp.where(live, beta_one * old_first + (1.0 - beta_one) * rotated, old_first)
+            out_v[2, rows, cols] = jnp.where(
+                live, beta_one * old_second + (1.0 - beta_one) * rotated * rotated, old_second)
+            out_v[3, rows, cols] = step
+        for copy in copies(i):
+            copy.start()
+        return carry
+
+    lax.fori_loop(0, W // STRIP, strip, 0)
+    for i in range(W // STRIP):
+        for copy in copies(i):
+            copy.wait()
 
 
 def call_store(touched, rot, direction, weights, first, second):
-    def slot(b, touched):
-        seen = jnp.int32(0)
-        for i in range(GRP - 1):
-            seen = seen + jnp.where((i < b) & (touched[i] > 0), jnp.int32(1), jnp.int32(0))
-        return jnp.minimum(seen, SLOTS - 1), 0, 0
-
-    compact = pl.BlockSpec((1, W, BLK), slot)
-    block = pl.BlockSpec((W, BLK), lambda b, touched: (0, b))
+    vmem = pl.BlockSpec(memory_space=pltpu.VMEM)
     full = jax.ShapeDtypeStruct((W, GRP * BLK), jnp.float32)
     return pl.pallas_call(
         store,
         out_shape=(full,) * 4,
-        grid_spec=pltpu.PrefetchScalarGridSpec(
-            num_scalar_prefetch=1, grid=(GRP,), in_specs=[compact] * 2 + [block] * 3, out_specs=[block] * 4),
+        in_specs=[pl.BlockSpec(memory_space=pltpu.SMEM)] + [vmem] * 5,
+        out_specs=[pl.BlockSpec(memory_space=pl.ANY)] * 4,
+        scratch_shapes=[pltpu.VMEM((4, W, GRP * BLK), jnp.float32), pltpu.SemaphoreType.DMA((4, W // STRIP))],
+        compiler_params=pltpu.CompilerParams(vmem_limit_bytes=32 * 2**20),
         name="store",
     )(touched, rot, direction, weights, first, second)
 

time: 93.3 us -> 84.5 us (0.906)
  Pallas kernels: 92.3 us -> 83.7 us
    pallas_call x1, Pallas kernels: 9.29 us -> 3.92 us  [call_store(): pl.pallas_call(store, out_shape=(full,) * 4, in_specs=[pl.BlockSpec(memor...]
    pallas_call x1, Pallas kernels: 83.1 us -> 79.7 us  [call_exchange(): pl.pallas_call(exchange, out_shape=(compact, compact), in_specs=[pl.Block...]
where the time goes in v2:
time: 84.5 us; the launch traced here: 84.4 us
  Pallas kernels  83.7 us (99%)
    pallas_call x1, Pallas kernels, call_exchange(): pl.pallas_call(exchange, out_shape=(compact, compact), in_specs=[pl.Block...  79.7 us
    pallas_call x1, Pallas kernels, call_store(): pl.pallas_call(store, out_shape=(full,) * 4, in_specs=[pl.BlockSpec(memor...  3.92 us

profile of v2, /device:TPU:0, one launch (start us, length us, event | category | flops | bytes accessed | tf_op | source)
XLA Modules:
  0.0 84.4 jit_solution(3622849240250884994)
XLA Ops:
  0.6 0.0 copy-start
  0.6 0.0 copy-start.1
  0.7 0.0 copy-start.2
  0.7 0.0 copy-start.3
  0.7 79.7 %exchange.1 = (f32[4,448,128]{2,1,0:T(8,128)S(1)}, f32[4,448,128]{2,1,0:T(8,128)S(1)}) custom-call(s32[8]{0:T(128)} %touched.3, bf16[448,1024]{1,0:T(8,128)(2,1)} %bitcast.19, f32[448,1024]{1,0:T(8,128)} %bitcast.9, f32[448,1024]{1,0:T(8,128)} %bitcast.11, bf16[448,7168]{1,0:T(8,128)(2,1)} %bitcast.14), custom_call_target="tpu_custom_call" | custom-call | flops 6576668672 | bytes 16777216 | tf_op jit(solution)/shard_map/exchange/pallas_call | solution.py:400
  80.4 0.0 copy-done
  80.4 0.0 copy-done.1
  80.4 0.0 copy-done.2
  80.5 0.0 copy-done.3
  80.5 3.9 %store.1 = (f32[448,1024]{1,0:T(8,128)}, f32[448,1024]{1,0:T(8,128)}, f32[448,1024]{1,0:T(8,128)}, f32[448,1024]{1,0:T(8,128)}) custom-call(s32[8]{0:T(128)S(1)} %copy-done.3, f32[4,448,128]{2,1,0:T(8,128)S(1)} %get-tuple-element.10.rot, f32[4,448,128]{2,1,0:T(8,128)S(1)} %get-tuple-element.11.direction, f32[448,1024]{1,0:T(8,128)S(1)} %bitcast.13, ...), custom_call_target="tpu_custom_call" | custom-call | tf_op jit(solution)/shard_map/store/pallas_call | solution.py:452
Async XLA Ops:
  0.6 79.8 %copy-start = (f32[1024,448]{0,1:T(8,128)S(1)}, f32[1024,448]{0,1:T(8,128)}, u32[]{:S(2)}) copy-start(f32[1024,448]{0,1:T(8,128)} %param.8) | copy-start | bytes 5505028
  0.6 79.8 %copy-start.1 = (f32[1024,448]{0,1:T(8,128)S(1)}, f32[1024,448]{0,1:T(8,128)}, u32[]{:S(2)}) copy-start(f32[1024,448]{0,1:T(8,128)} %param.9) | copy-start | bytes 5505028
  0.7 79.8 %copy-start.2 = (f32[1024,448]{0,1:T(8,128)S(1)}, f32[1024,448]{0,1:T(8,128)}, u32[]{:S(2)}) copy-start(f32[1024,448]{0,1:T(8,128)} %param.6) | copy-start | bytes 5505028
  0.7 79.8 %copy-start.3 = (s32[8]{0:T(128)S(1)}, s32[8]{0:T(128)}, u32[]{:S(2)}) copy-start(s32[8]{0:T(128)} %touched.3) | copy-start | bytes 100

commit v3 on v2

--- a/solution.py
+++ b/solution.py
@@ -15,8 +15,7 @@
 HALF = W // 2
 PART = W // 4
 KPART = K // 2
-DIRECT = 80
-VIA = (PART - DIRECT) // 2
+DIRECT = 96
 SUBS = ((0, 64), (64, 48))
 PAIR = 2
 STRIP = 64
@@ -46,7 +45,7 @@
 
 
 def exchange(touched, grad_hbm, first_hbm, second_hbm, basis_hbm, rot_out, dir_out,
-             grad_v, first_v, second_v, first_c, second_c, basis_v, gw, nw, own_v, back_v,
+             grad_v, first_v, second_v, first_c, second_c, basis_v, gw, nw, own_v, near_v, back_v,
              xs2, xa, xs, xr, ys2, ya, ys, yr,
              load_sem,
              bx_s, bx_r, bz_s, bz_r, bf_s, bf_r, bc_s, bc_r,
@@ -64,10 +63,10 @@
 
     xp, xm, x2 = device(dx=1), device(dx=3), device(dx=2)
     yp, ym = device(dy=1), device(dy=3)
-    zp, zm, other = device(dz=1), device(dz=3), device(dc=1)
+    zp, zm, z2, other = device(dz=1), device(dz=3), device(dz=2), device(dc=1)
 
     barrier = pltpu.get_barrier_semaphore()
-    peers = (xp, xm, x2, yp, ym, zp, zm, other)
+    peers = (xp, xm, x2, yp, ym, zp, zm, z2, other)
     for peer in peers:
         pl.semaphore_signal(barrier, inc=1, device_id=peer, device_id_type=MESH)
 
@@ -109,13 +108,13 @@
         piece = part(ring_of(x, d), 3 if up else 1, c, *SUBS[n])
         return remote(piece, piece, bz_s.at[d - 1, up, n], bz_r.at[d - 1, up, n], zp if up else zm)
 
-    def bf(d, up):
-        piece = part(ring_of(x, d), 3 if up else 1, c, DIRECT + up * VIA, VIA)
-        return remote(piece, piece, bf_s.at[d - 1, up], bf_r.at[d - 1, up], zp if up else zm)
-
-    def bf_in(d, up):
-        piece = part(ring_of(x, d), 2, c, DIRECT + up * VIA, VIA)
-        return remote(piece, piece, bf_s.at[d - 1, up], bf_r.at[d - 1, up], zp if up else zm)
+    def bf(d):
+        piece = part(ring_of(x, d), 0, c, DIRECT, PART - DIRECT)
+        return remote(piece, piece, bf_s.at[d - 1], bf_r.at[d - 1], z2)
+
+    def bf_in(d):
+        piece = part(ring_of(x, d), 2, c, DIRECT, PART - DIRECT)
+        return remote(piece, piece, bf_s.at[d - 1], bf_r.at[d - 1], z2)
 
     def bc_span(k, n):
         return (0, PART) if k == 2 else SUBS[n]
@@ -191,19 +190,18 @@
         bx_in(d, n).wait_recv()
         bz(d, 1, n).start()
         bz(d, 0, n).start()
+        if n:
+            bf(d).start()
         bc(d, 0, n).start()
 
     def pass_round(d, n):
         for up, k in ((0, 1), (1, 3)):
             bz_in(d, up, n).wait_recv()
-            if n:
-                bf(d, up).start()
             bc(d, k, n).start()
 
     def pass_last(d):
         bx_in(d, 2).wait_recv()
-        bf_in(d, 0).wait_recv()
-        bf_in(d, 1).wait_recv()
+        bf_in(d).wait_recv()
         bc(d, 2).start()
 
     def whole(d):
@@ -248,60 +246,29 @@
             near(j, up, 1).wait_recv()
         return term + t[0, j].astype(jnp.float32) + t[1, j].astype(jnp.float32)
 
-    pass_on(2, 0)
-    forward_g(0)
-    send_g(2)
-    pass_on(2, 1)
-    forward_g(1)
-    send_g(3)
-    for load in loads[2:]:
-        load.wait()
-    for j in range(SLOTS):
-        first_c[j] = live_block(slots, j, first_v)
-        second_c[j] = live_block(slots, j, second_v)
-    pass_on(3, 0)
-    pass_on(1, 0)
-    pass_round(2, 0)
-    pass_round(2, 1)
-    for dx in (2, 1, 3):
-        bx(dx, 2).start()
-    pass_on(3, 1)
-    pass_on(1, 1)
-    forward_g(2)
-    forward_g(3)
-    pass_last(2)
-    pass_round(3, 0)
-    pass_round(1, 0)
-    loads[1].wait()
-    whole(2)
-
-    def step_far(i):
-        for t in range(PAIR):
-            arrived_g(i * PAIR + t)
+    def far_pair(i):
         share = rotate(2, i)
         for t in range(PAIR):
             send_far(share[:, t * BLK:(t + 1) * BLK], xs2, x_far, i * PAIR + t)
+
+    def own_pair(i):
         share = rotate(0, i)
         for t in range(PAIR):
             own_v[i * PAIR + t] = share[:, t * BLK:(t + 1) * BLK]
 
-    loop(step_far, SLOTS // PAIR)
-    pass_round(3, 1)
-    pass_round(1, 1)
-    pass_last(1)
-    pass_last(3)
-    whole(3)
-    whole(1)
-
-    def step_near(i):
-        for d, up in ((3, 0), (1, 1)):
-            share = rotate(d, i)
-            for t in range(PAIR):
-                send_ready(share[:, t * BLK:(t + 1) * BLK], up, xs, x_near, i * PAIR + t)
-            for t in range(PAIR):
-                send_summed(share[:, t * BLK:(t + 1) * BLK], up, xa, xs, x_far, x_near, i * PAIR + t)
-
-    loop(step_near, SLOTS // PAIR)
+    def near(j):
+        @pl.when(lax.rem(j, PAIR) == 0)
+        def _():
+            for d, up in ((3, 0), (1, 1)):
+                share = rotate(d, j // PAIR)
+                for t in range(PAIR):
+                    near_v[up, t] = share[:, t * BLK:(t + 1) * BLK]
+
+        t = lax.rem(j, PAIR)
+        for up in (0, 1):
+            send_ready(near_v[up, t], up, xs, x_near, j)
+        for up in (0, 1):
+            send_summed(near_v[up, t], up, xa, xs, x_far, x_near, j)
 
     def normalise(j):
         rotated = finish(own_v[j], xr, x_near, j)
@@ -338,7 +305,48 @@
     def back_own(j):
         dir_out[j] = finish(back_v[j, y], yr, y_near, j)
 
-    tasks = (normalise, forward_n, back_far, back_near, back_own)
+    pass_on(2, 0)
+    forward_g(0)
+    send_g(2)
+    pass_on(2, 1)
+    forward_g(1)
+    send_g(3)
+    for dx in (2, 1, 3):
+        bx(dx, 2).start()
+    for load in loads[2:]:
+        load.wait()
+    for j in range(SLOTS):
+        first_c[j] = live_block(slots, j, first_v)
+        second_c[j] = live_block(slots, j, second_v)
+    pass_on(3, 0)
+    pass_on(1, 0)
+    pass_round(2, 0)
+    pass_on(3, 1)
+    pass_on(1, 1)
+    pass_round(2, 1)
+    loads[1].wait()
+    forward_g(2)
+    arrived_g(0)
+    arrived_g(1)
+    own_pair(0)
+    forward_g(3)
+    pass_last(2)
+    pass_round(3, 0)
+    pass_round(1, 0)
+    whole(2)
+    far_pair(0)
+    pass_round(3, 1)
+    pass_round(1, 1)
+    arrived_g(2)
+    arrived_g(3)
+    far_pair(1)
+    pass_last(3)
+    pass_last(1)
+    own_pair(1)
+    whole(3)
+    whole(1)
+
+    tasks = (near, normalise, forward_n, back_far, back_near, back_own)
 
     def skewed(t):
         for lag, task in enumerate(tasks):
@@ -356,11 +364,11 @@
         for up in (0, 1):
             bz(d, up, 0).wait_send()
             bz(d, up, 1).wait_send()
-            bf(d, up).wait_send()
         for k in (0, 1, 3):
             bc(d, k, 0).wait_send()
             bc(d, k, 1).wait_send()
         bc(d, 2).wait_send()
+        bf(d).wait_send()
 
     def drain(j):
         for up in (0, 1):
@@ -390,10 +398,10 @@
         pltpu.VMEM((SLOTS, W, BLK), f32), pltpu.VMEM((SLOTS, W, BLK), f32),
         pltpu.VMEM((RING, W, K), bf16),
         pltpu.VMEM((SLOTS, RING, W, BLK), bf16), pltpu.VMEM((SLOTS, RING, W, BLK), bf16),
-        pltpu.VMEM((SLOTS, W, BLK), f32), pltpu.VMEM((SLOTS, RING, W, BLK), f32),
+        pltpu.VMEM((SLOTS, W, BLK), f32), pltpu.VMEM((2, PAIR, W, BLK), f32), pltpu.VMEM((SLOTS, RING, W, BLK), f32),
         *sum_buffers(), *sum_buffers(),
         pltpu.SemaphoreType.DMA((4,)),
-        *sems(3, 3), *sems(3, 2, 2), *sems(3, 2), *sems(3, 4, 2),
+        *sems(3, 3), *sems(3, 2, 2), *sems(3), *sems(3, 4, 2),
         *sems(4, SLOTS), *sems(4, SLOTS), *sems(6, SLOTS), *sems(6, SLOTS),
     ]
     compact = pltpu.VMEM((SLOTS, W, BLK), f32)

time: 84.5 us -> 80.1 us (0.948)
  Pallas kernels: 83.7 us -> 79.3 us
    pallas_call x1, Pallas kernels: 79.7 us -> 75.3 us  [call_exchange(): pl.pallas_call(exchange, out_shape=(compact, compact), in_specs=[pl.Block...]
where the time goes in v3:
time: 80.1 us; the launch traced here: 80 us
  Pallas kernels  79.3 us (99%)
    pallas_call x1, Pallas kernels, call_exchange(): pl.pallas_call(exchange, out_shape=(compact, compact), in_specs=[pl.Block...  75.3 us
    pallas_call x1, Pallas kernels, call_store(): pl.pallas_call(store, out_shape=(full,) * 4, in_specs=[pl.BlockSpec(memor...  3.92 us

profile of v3, /device:TPU:0, one launch (start us, length us, event | category | flops | bytes accessed | tf_op | source)
XLA Modules:
  0.0 80.0 jit_solution(3744587733992474566)
XLA Ops:
  0.6 0.0 copy-start
  0.6 0.0 copy-start.1
  0.7 0.0 copy-start.2
  0.7 0.0 copy-start.3
  0.7 75.3 %exchange.1 = (f32[4,448,128]{2,1,0:T(8,128)S(1)}, f32[4,448,128]{2,1,0:T(8,128)S(1)}) custom-call(s32[8]{0:T(128)} %touched.3, bf16[448,1024]{1,0:T(8,128)(2,1)} %bitcast.19, f32[448,1024]{1,0:T(8,128)} %bitcast.9, f32[448,1024]{1,0:T(8,128)} %bitcast.11, bf16[448,7168]{1,0:T(8,128)(2,1)} %bitcast.14), custom_call_target="tpu_custom_call" | custom-call | flops 6576668672 | bytes 16777216 | tf_op jit(solution)/shard_map/exchange/pallas_call | solution.py:408
  76.0 0.0 copy-done
  76.0 0.0 copy-done.1
  76.0 0.0 copy-done.2
  76.1 0.0 copy-done.3
  76.1 3.9 %store.1 = (f32[448,1024]{1,0:T(8,128)}, f32[448,1024]{1,0:T(8,128)}, f32[448,1024]{1,0:T(8,128)}, f32[448,1024]{1,0:T(8,128)}) custom-call(s32[8]{0:T(128)S(1)} %copy-done.3, f32[4,448,128]{2,1,0:T(8,128)S(1)} %get-tuple-element.10.rot, f32[4,448,128]{2,1,0:T(8,128)S(1)} %get-tuple-element.11.direction, f32[448,1024]{1,0:T(8,128)S(1)} %bitcast.13, ...), custom_call_target="tpu_custom_call" | custom-call | tf_op jit(solution)/shard_map/store/pallas_call | solution.py:460
Async XLA Ops:
  0.6 75.4 %copy-start = (f32[1024,448]{0,1:T(8,128)S(1)}, f32[1024,448]{0,1:T(8,128)}, u32[]{:S(2)}) copy-start(f32[1024,448]{0,1:T(8,128)} %param.8) | copy-start | bytes 5505028
  0.6 75.4 %copy-start.1 = (f32[1024,448]{0,1:T(8,128)S(1)}, f32[1024,448]{0,1:T(8,128)}, u32[]{:S(2)}) copy-start(f32[1024,448]{0,1:T(8,128)} %param.9) | copy-start | bytes 5505028
  0.7 75.4 %copy-start.2 = (f32[1024,448]{0,1:T(8,128)S(1)}, f32[1024,448]{0,1:T(8,128)}, u32[]{:S(2)}) copy-start(f32[1024,448]{0,1:T(8,128)} %param.6) | copy-start | bytes 5505028
  0.7 75.4 %copy-start.3 = (s32[8]{0:T(128)S(1)}, s32[8]{0:T(128)}, u32[]{:S(2)}) copy-start(s32[8]{0:T(128)} %touched.3) | copy-start | bytes 100

commit v4 on v3

--- a/solution.py
+++ b/solution.py
@@ -15,7 +15,6 @@
 HALF = W // 2
 PART = W // 4
 KPART = K // 2
-DIRECT = 96
 SUBS = ((0, 64), (64, 48))
 PAIR = 2
 STRIP = 64
@@ -48,7 +47,7 @@
              grad_v, first_v, second_v, first_c, second_c, basis_v, gw, nw, own_v, near_v, back_v,
              xs2, xa, xs, xr, ys2, ya, ys, yr,
              load_sem,
-             bx_s, bx_r, bz_s, bz_r, bf_s, bf_r, bc_s, bc_r,
+             bx_s, bx_r, bz_s, bz_r, bc_s, bc_r,
              gy_s, gy_r, nx_s, nx_r, rx_s, rx_r, ry_s, ry_r):
     r, p = lax.axis_index("rows"), lax.axis_index("panel")
     z, c = r // 2, lax.rem(r, 2)
@@ -63,10 +62,10 @@
 
     xp, xm, x2 = device(dx=1), device(dx=3), device(dx=2)
     yp, ym = device(dy=1), device(dy=3)
-    zp, zm, z2, other = device(dz=1), device(dz=3), device(dz=2), device(dc=1)
+    zp, zm, other = device(dz=1), device(dz=3), device(dc=1)
 
     barrier = pltpu.get_barrier_semaphore()
-    peers = (xp, xm, x2, yp, ym, zp, zm, z2, other)
+    peers = (xp, xm, x2, yp, ym, zp, zm, other)
     for peer in peers:
         pl.semaphore_signal(barrier, inc=1, device_id=peer, device_id_type=MESH)
 
@@ -86,7 +85,7 @@
         return basis_v.at[panel, rows, pl.ds(pl.multiple_of(core * KPART, 128), KPART)]
 
     def span(n):
-        return (0, *SUBS[n]) if n < 2 else (2, 0, DIRECT)
+        return (0, *SUBS[n]) if n < 2 else (2, 0, PART)
 
     def bx(dx, n):
         k, low, size = span(n)
@@ -107,14 +106,6 @@
     def bz_in(d, up, n):
         piece = part(ring_of(x, d), 3 if up else 1, c, *SUBS[n])
         return remote(piece, piece, bz_s.at[d - 1, up, n], bz_r.at[d - 1, up, n], zp if up else zm)
-
-    def bf(d):
-        piece = part(ring_of(x, d), 0, c, DIRECT, PART - DIRECT)
-        return remote(piece, piece, bf_s.at[d - 1], bf_r.at[d - 1], z2)
-
-    def bf_in(d):
-        piece = part(ring_of(x, d), 2, c, DIRECT, PART - DIRECT)
-        return remote(piece, piece, bf_s.at[d - 1], bf_r.at[d - 1], z2)
 
     def bc_span(k, n):
         return (0, PART) if k == 2 else SUBS[n]
@@ -190,8 +181,6 @@
         bx_in(d, n).wait_recv()
         bz(d, 1, n).start()
         bz(d, 0, n).start()
-        if n:
-            bf(d).start()
         bc(d, 0, n).start()
 
     def pass_round(d, n):
@@ -201,7 +190,6 @@
 
     def pass_last(d):
         bx_in(d, 2).wait_recv()
-        bf_in(d).wait_recv()
         bc(d, 2).start()
 
     def whole(d):
@@ -368,7 +356,6 @@
             bc(d, k, 0).wait_send()
             bc(d, k, 1).wait_send()
         bc(d, 2).wait_send()
-        bf(d).wait_send()
 
     def drain(j):
         for up in (0, 1):
@@ -401,7 +388,7 @@
         pltpu.VMEM((SLOTS, W, BLK), f32), pltpu.VMEM((2, PAIR, W, BLK), f32), pltpu.VMEM((SLOTS, RING, W, BLK), f32),
         *sum_buffers(), *sum_buffers(),
         pltpu.SemaphoreType.DMA((4,)),
-        *sems(3, 3), *sems(3, 2, 2), *sems(3), *sems(3, 4, 2),
+        *sems(3, 3), *sems(3, 2, 2), *sems(3, 4, 2),
         *sems(4, SLOTS), *sems(4, SLOTS), *sems(6, SLOTS), *sems(6, SLOTS),
     ]
     compact = pltpu.VMEM((SLOTS, W, BLK), f32)

time: 80.1 us -> 78.5 us (0.980)
  Pallas kernels: 79.3 us -> 77.7 us
    pallas_call x1, Pallas kernels: 75.3 us -> 73.7 us  [call_exchange(): pl.pallas_call(exchange, out_shape=(compact, compact), in_specs=[pl.Block...]
where the time goes in v4:
time: 78.5 us; the launch traced here: 78.4 us
  Pallas kernels  77.7 us (99%)
    pallas_call x1, Pallas kernels, call_exchange(): pl.pallas_call(exchange, out_shape=(compact, compact), in_specs=[pl.Block...  73.7 us
    pallas_call x1, Pallas kernels, call_store(): pl.pallas_call(store, out_shape=(full,) * 4, in_specs=[pl.BlockSpec(memor...  3.92 us

profile of v4, /device:TPU:0, one launch (start us, length us, event | category | flops | bytes accessed | tf_op | source)
XLA Modules:
  0.0 78.4 jit_solution(5440616197934408002)
XLA Ops:
  0.6 0.0 copy-start
  0.6 0.0 copy-start.1
  0.7 0.0 copy-start.2
  0.7 0.0 copy-start.3
  0.7 73.7 %exchange.1 = (f32[4,448,128]{2,1,0:T(8,128)S(1)}, f32[4,448,128]{2,1,0:T(8,128)S(1)}) custom-call(s32[8]{0:T(128)} %touched.3, bf16[448,1024]{1,0:T(8,128)(2,1)} %bitcast.19, f32[448,1024]{1,0:T(8,128)} %bitcast.9, f32[448,1024]{1,0:T(8,128)} %bitcast.11, bf16[448,7168]{1,0:T(8,128)(2,1)} %bitcast.14), custom_call_target="tpu_custom_call" | custom-call | flops 6576668672 | bytes 16777216 | tf_op jit(solution)/shard_map/exchange/pallas_call | solution.py:395
  74.4 0.0 copy-done
  74.4 0.0 copy-done.1
  74.4 0.0 copy-done.2
  74.5 0.0 copy-done.3
  74.5 3.9 %store.1 = (f32[448,1024]{1,0:T(8,128)}, f32[448,1024]{1,0:T(8,128)}, f32[448,1024]{1,0:T(8,128)}, f32[448,1024]{1,0:T(8,128)}) custom-call(s32[8]{0:T(128)S(1)} %copy-done.3, f32[4,448,128]{2,1,0:T(8,128)S(1)} %get-tuple-element.10.rot, f32[4,448,128]{2,1,0:T(8,128)S(1)} %get-tuple-element.11.direction, f32[448,1024]{1,0:T(8,128)S(1)} %bitcast.13, ...), custom_call_target="tpu_custom_call" | custom-call | tf_op jit(solution)/shard_map/store/pallas_call | solution.py:447
Async XLA Ops:
  0.6 73.8 %copy-start = (f32[1024,448]{0,1:T(8,128)S(1)}, f32[1024,448]{0,1:T(8,128)}, u32[]{:S(2)}) copy-start(f32[1024,448]{0,1:T(8,128)} %param.8) | copy-start | bytes 5505028
  0.6 73.8 %copy-start.1 = (f32[1024,448]{0,1:T(8,128)S(1)}, f32[1024,448]{0,1:T(8,128)}, u32[]{:S(2)}) copy-start(f32[1024,448]{0,1:T(8,128)} %param.9) | copy-start | bytes 5505028
  0.7 73.8 %copy-start.2 = (f32[1024,448]{0,1:T(8,128)S(1)}, f32[1024,448]{0,1:T(8,128)}, u32[]{:S(2)}) copy-start(f32[1024,448]{0,1:T(8,128)} %param.6) | copy-start | bytes 5505028
  0.7 73.8 %copy-start.3 = (s32[8]{0:T(128)S(1)}, s32[8]{0:T(128)}, u32[]{:S(2)}) copy-start(s32[8]{0:T(128)} %touched.3) | copy-start | bytes 100

commit v5 on v4

--- a/solution.py
+++ b/solution.py
@@ -44,7 +44,7 @@
 
 
 def exchange(touched, grad_hbm, first_hbm, second_hbm, basis_hbm, rot_out, dir_out,
-             grad_v, first_v, second_v, first_c, second_c, basis_v, gw, nw, own_v, near_v, back_v,
+             grad_v, first_v, second_v, first_c, second_c, basis_v, gw, nw, nt, own_v, near_v, back_v,
              xs2, xa, xs, xr, ys2, ya, ys, yr,
              load_sem,
              bx_s, bx_r, bz_s, bz_r, bc_s, bc_r,
@@ -85,7 +85,7 @@
         return basis_v.at[panel, rows, pl.ds(pl.multiple_of(core * KPART, 128), KPART)]
 
     def span(n):
-        return (0, *SUBS[n]) if n < 2 else (2, 0, PART)
+        return (2 * (n // 2), *SUBS[n % 2])
 
     def bx(dx, n):
         k, low, size = span(n)
@@ -108,7 +108,7 @@
         return remote(piece, piece, bz_s.at[d - 1, up, n], bz_r.at[d - 1, up, n], zp if up else zm)
 
     def bc_span(k, n):
-        return (0, PART) if k == 2 else SUBS[n]
+        return SUBS[n]
 
     def bc(d, k, n=0):
         piece = part(ring_of(x, d), k, c, *bc_span(k, n))
@@ -189,14 +189,14 @@
             bc(d, k, n).start()
 
     def pass_last(d):
-        bx_in(d, 2).wait_recv()
-        bc(d, 2).start()
+        for n in (0, 1):
+            bx_in(d, 2 + n).wait_recv()
+            bc(d, 2, n).start()
 
     def whole(d):
         for n in (0, 1):
-            for k in (0, 1, 3):
+            for k in (0, 1, 3, 2):
                 bc_in(d, k, n).wait_recv()
-        bc_in(d, 2).wait_recv()
 
     def forward_g(j):
         g_own_in(j, 0).wait_recv()
@@ -277,12 +277,23 @@
     def back_far(j):
         n_on_in(j, 0).wait_recv()
         n_on_in(j, 1).wait_recv()
-        total = None
         for d in range(RING):
-            term = jnp.dot(nw[j, d].T, basis_v[d], preferred_element_type=jnp.float32)
-            total = term if total is None else total + term
-        back_v[j] = total.T.reshape(RING, W, BLK)
-        send_far(back_v[j, ring_of(y, 2)], ys2, y_far, j)
+            nt[d] = nw[j, d].T
+
+        def half(n):
+            which = lax.rem(ring_of(y, 2) // 2 + n, 2)
+            cols = pl.ds(pl.multiple_of(which * KPART, 128), KPART)
+            total = None
+            for d in range(RING):
+                term = jnp.dot(nt[d], basis_v[d, :, cols], preferred_element_type=jnp.float32)
+                total = term if total is None else total + term
+            back_v[j, pl.ds(which * 2, 2)] = total.T.reshape(2, W, BLK)
+
+            @pl.when(n == 0)
+            def _():
+                send_far(back_v[j, ring_of(y, 2)], ys2, y_far, j)
+
+        loop(half, 2)
         send_ready(back_v[j, ring_of(y, 3)], 0, ys, y_near, j)
         send_ready(back_v[j, ring_of(y, 1)], 1, ys, y_near, j)
 
@@ -301,11 +312,7 @@
     send_g(3)
     for dx in (2, 1, 3):
         bx(dx, 2).start()
-    for load in loads[2:]:
-        load.wait()
-    for j in range(SLOTS):
-        first_c[j] = live_block(slots, j, first_v)
-        second_c[j] = live_block(slots, j, second_v)
+        bx(dx, 3).start()
     pass_on(3, 0)
     pass_on(1, 0)
     pass_round(2, 0)
@@ -323,6 +330,11 @@
     pass_round(1, 0)
     whole(2)
     far_pair(0)
+    for load in loads[2:]:
+        load.wait()
+    for j in range(SLOTS):
+        first_c[j] = live_block(slots, j, first_v)
+        second_c[j] = live_block(slots, j, second_v)
     pass_round(3, 1)
     pass_round(1, 1)
     arrived_g(2)
@@ -347,15 +359,14 @@
     loop(skewed, SLOTS + len(tasks) - 1)
 
     for d in (2, 1, 3):
-        for n in range(3):
+        for n in range(4):
             bx(d, n).wait_send()
         for up in (0, 1):
             bz(d, up, 0).wait_send()
             bz(d, up, 1).wait_send()
-        for k in (0, 1, 3):
+        for k in range(4):
             bc(d, k, 0).wait_send()
             bc(d, k, 1).wait_send()
-        bc(d, 2).wait_send()
 
     def drain(j):
         for up in (0, 1):
@@ -385,10 +396,11 @@
         pltpu.VMEM((SLOTS, W, BLK), f32), pltpu.VMEM((SLOTS, W, BLK), f32),
         pltpu.VMEM((RING, W, K), bf16),
         pltpu.VMEM((SLOTS, RING, W, BLK), bf16), pltpu.VMEM((SLOTS, RING, W, BLK), bf16),
+        pltpu.VMEM((RING, BLK, W), bf16),
         pltpu.VMEM((SLOTS, W, BLK), f32), pltpu.VMEM((2, PAIR, W, BLK), f32), pltpu.VMEM((SLOTS, RING, W, BLK), f32),
         *sum_buffers(), *sum_buffers(),
         pltpu.SemaphoreType.DMA((4,)),
-        *sems(3, 3), *sems(3, 2, 2), *sems(3, 4, 2),
+        *sems(3, 4), *sems(3, 2, 2), *sems(3, 4, 2),
         *sems(4, SLOTS), *sems(4, SLOTS), *sems(6, SLOTS), *sems(6, SLOTS),
     ]
     compact = pltpu.VMEM((SLOTS, W, BLK), f32)

time: 78.5 us -> 78.3 us (level)
  no operation moved by 1% of the time
where the time goes in v5:
time: 78.3 us; the launch traced here: 78.2 us
  Pallas kernels  77.5 us (99%)
    pallas_call x1, Pallas kernels, call_exchange(): pl.pallas_call(exchange, out_shape=(compact, compact), in_specs=[pl.Block...  73.6 us
    pallas_call x1, Pallas kernels, call_store(): pl.pallas_call(store, out_shape=(full,) * 4, in_specs=[pl.BlockSpec(memor...  3.92 us

profile of v5, /device:TPU:0, one launch (start us, length us, event | category | flops | bytes accessed | tf_op | source)
XLA Modules:
  0.0 78.2 jit_solution(7319295788620300191)
XLA Ops:
  0.6 0.0 copy-start
  0.6 0.0 copy-start.1
  0.7 0.0 copy-start.2
  0.7 0.0 copy-start.3
  0.7 73.6 %exchange.1 = (f32[4,448,128]{2,1,0:T(8,128)S(1)}, f32[4,448,128]{2,1,0:T(8,128)S(1)}) custom-call(s32[8]{0:T(128)} %touched.3, bf16[448,1024]{1,0:T(8,128)(2,1)} %bitcast.19, f32[448,1024]{1,0:T(8,128)} %bitcast.9, f32[448,1024]{1,0:T(8,128)} %bitcast.11, bf16[448,7168]{1,0:T(8,128)(2,1)} %bitcast.14), custom_call_target="tpu_custom_call" | custom-call | flops 6576668672 | bytes 16777216 | tf_op jit(solution)/shard_map/exchange/pallas_call | solution.py:407
  74.3 0.0 copy-done
  74.3 0.0 copy-done.1
  74.3 0.0 copy-done.2
  74.3 0.0 copy-done.3
  74.3 3.9 %store.1 = (f32[448,1024]{1,0:T(8,128)}, f32[448,1024]{1,0:T(8,128)}, f32[448,1024]{1,0:T(8,128)}, f32[448,1024]{1,0:T(8,128)}) custom-call(s32[8]{0:T(128)S(1)} %copy-done.3, f32[4,448,128]{2,1,0:T(8,128)S(1)} %get-tuple-element.10.rot, f32[4,448,128]{2,1,0:T(8,128)S(1)} %get-tuple-element.11.direction, f32[448,1024]{1,0:T(8,128)S(1)} %bitcast.13, ...), custom_call_target="tpu_custom_call" | custom-call | tf_op jit(solution)/shard_map/store/pallas_call | solution.py:459
Async XLA Ops:
  0.6 73.6 %copy-start = (f32[1024,448]{0,1:T(8,128)S(1)}, f32[1024,448]{0,1:T(8,128)}, u32[]{:S(2)}) copy-start(f32[1024,448]{0,1:T(8,128)} %param.8) | copy-start | bytes 5505028
  0.6 73.6 %copy-start.1 = (f32[1024,448]{0,1:T(8,128)S(1)}, f32[1024,448]{0,1:T(8,128)}, u32[]{:S(2)}) copy-start(f32[1024,448]{0,1:T(8,128)} %param.9) | copy-start | bytes 5505028
  0.7 73.6 %copy-start.2 = (f32[1024,448]{0,1:T(8,128)S(1)}, f32[1024,448]{0,1:T(8,128)}, u32[]{:S(2)}) copy-start(f32[1024,448]{0,1:T(8,128)} %param.6) | copy-start | bytes 5505028
  0.7 73.6 %copy-start.3 = (s32[8]{0:T(128)S(1)}, s32[8]{0:T(128)}, u32[]{:S(2)}) copy-start(s32[8]{0:T(128)} %touched.3) | copy-start | bytes 100
